TPU v7x, 512 devices: a whole 4x4x16 slice. The times are simulated.
512 devices in a mesh: ctx: 64 (over y, z), ch: 8 (over x, core).
Axes of the slice: x: 4, y: 4, z: 16, core: 2. Of those that a mesh axis runs over, the one named last changes fastest.
Arguments:
- query_rows: bfloat16 [8192, 8192], P('ctx', 'ch'), may hold values from -6 to 6
- key_rows: bfloat16 [8192, 8192], P('ctx', 'ch'), may hold values from -6 to 6
- value_rows: bfloat16 [8192, 8192], P('ctx', 'ch'), may hold values from -6 to 6
- short_filter: float32 [3, 3, 8192], P(None, None, 'ch'), may hold values from -3.5 to 3.5
- decay_rate: float32 [8192, 16], P('ch'), may hold values from 2e-05 to 0.1
- residues: float32 [8192, 16], P('ch'), may hold values from -1.5 to 1.5
- out_weight: bfloat16 [8192, 4096], P('ctx', 'ch'), may hold values from -0.1875 to 0.1875
- record_starts: int32 [4], replicated, may hold values from 0 to 8191, as said below
Outputs:
- block_out: bfloat16 [8192, 4096], P('ctx', 'ch')
Inputs may be any that keep to these rules, and one draw needn't show every extreme that they name: record_starts[0] is 0 and the last entry is 8191; the entries are distinct and increasing, and all but the first lie in the second half of the 8192 tokens.
All inputs are finite; a program needn't handle non-finite values.
Results may differ from a plain program's by a relative error of at most 0.017.
Values may be sent and summed in bfloat16 or wider, within the bound.
A program may use at most 64 MiB of HBM per device.

v0:
```python
import jax
import jax.numpy as jnp
from jax import lax
from jax.sharding import PartitionSpec as P

MODES = 16
KS = 3


def shifted(block, axis, distance):
    devices = range(lax.axis_size(axis))
    route = [(i - distance, i) for i in devices if i - distance in devices]
    return lax.ppermute(block, axis, route)


def carried_in(x, axis, combine, identity):
    devices, mine = (lax.axis_size(axis), lax.axis_index(axis))
    everything = jax.tree.map(lambda part: lax.all_gather(part, axis), x)
    start = jax.tree.map(
        lambda part, zero: jnp.broadcast_to(jnp.asarray(zero, part.dtype), part.shape), x, identity
    )

    def hop(k, before):
        reached = k < mine
        new = combine(before, jax.tree.map(lambda part: part[k], everything))
        return jax.tree.map(lambda a, b: jnp.where(reached, a, b), new, before)

    return lax.fori_loop(0, devices, hop, start)


def ages_of(positions, record_starts):
    earlier = record_starts[None, :] <= positions[:, None]
    segment = jnp.max(jnp.where(earlier, record_starts[None, :], 0), axis=1)
    return positions - segment


def masked_conv(extended, weights, ages, count):
    taps = weights.shape[0]
    total = jnp.zeros((count, extended.shape[1]), jnp.float32)
    for tap_index in range(taps):
        keeper = (ages >= tap_index).astype(jnp.float32)[:, None]
        window = extended[taps - 1 - tap_index : taps - 1 - tap_index + count]
        total = total + weights[tap_index][None, :] * window * keeper
    return total


def combine_pairs(earlier, later_pair):
    return (earlier[0] * later_pair[0], later_pair[0] * earlier[1] + later_pair[1])


def local(
    query_rows, key_rows, value_rows, short_filter, decay_rate, residues, out_weight, record_starts
):
    row_count, channels = query_rows.shape
    anchor = lax.axis_index("ctx") * row_count
    positions = anchor + jnp.arange(row_count, dtype=jnp.int32)
    ages = ages_of(positions, record_starts)
    reach_short = KS - 1
    tails = shifted(
        (
            query_rows[row_count - reach_short :],
            key_rows[row_count - reach_short :],
            value_rows[row_count - reach_short :],
        ),
        "ctx",
        1,
    )
    query_conv = masked_conv(
        jnp.concatenate([tails[0], query_rows], axis=0).astype(jnp.float32),
        short_filter[0],
        ages,
        row_count,
    )
    key_conv = masked_conv(
        jnp.concatenate([tails[1], key_rows], axis=0).astype(jnp.float32),
        short_filter[1],
        ages,
        row_count,
    )
    value_conv = masked_conv(
        jnp.concatenate([tails[2], value_rows], axis=0).astype(jnp.float32),
        short_filter[2],
        ages,
        row_count,
    )
    mixed = (key_conv * value_conv).astype(jnp.bfloat16).astype(jnp.float32)
    gain = jnp.sqrt(1.0 - jnp.exp(-2.0 * decay_rate))
    block_rows = 8
    block_count = row_count // block_rows
    inner_index = jnp.arange(block_rows, dtype=jnp.float32)
    inner_ints = jnp.arange(block_rows, dtype=jnp.int32)
    rising = jnp.exp(-decay_rate[None, :, :] * inner_index[:, None, None])
    taps_inner = jnp.sum(rising * (residues * gain)[None, :, :], axis=2)
    local_index = jnp.arange(row_count, dtype=jnp.int32)
    inner_ages = jnp.minimum(ages, local_index % block_rows)
    padded_mixed = jnp.concatenate(
        [jnp.zeros((block_rows - 1, channels), jnp.float32), mixed], axis=0
    )
    within = masked_conv(padded_mixed, taps_inner, inner_ages, row_count)
    entry_powers = jnp.exp(-decay_rate[None, :, :] * (inner_index[:, None, None] + 1.0))
    final_powers = (
        jnp.exp(-decay_rate[None, :, :] * (block_rows - 1.0 - inner_index[:, None, None]))
        * gain[None, :, :]
    )
    block_decay = jnp.exp(-decay_rate * block_rows)
    mixed_blocks = mixed.reshape(block_count, block_rows, channels)
    age_blocks = ages.reshape(block_count, block_rows)
    last_ages = age_blocks[:, block_rows - 1]
    weighted = (last_ages[:, None] >= block_rows - 1 - inner_ints[None, :]).astype(jnp.float32)
    endings = jnp.einsum("rcm,brc->bcm", final_powers, mixed_blocks * weighted[:, :, None])
    unbroken = (last_ages >= block_rows).astype(jnp.float32)

    def advance(state, inputs):
        ending, kept = inputs
        return (block_decay * kept * state + ending, state)

    local_state, entering_states = lax.scan(
        advance, jnp.zeros((channels, MODES), jnp.float32), (endings, unbroken)
    )
    entering = (age_blocks > inner_ints[None, :]).astype(jnp.float32)
    between = (
        jnp.einsum("rcm,bcm->brc", entry_powers, residues[None, :, :] * entering_states)
        * entering[:, :, None]
    )
    device_decay = jnp.exp(-decay_rate * row_count) * (ages[row_count - 1] >= row_count).astype(
        jnp.float32
    )
    identity_pair = (jnp.ones_like(device_decay), jnp.zeros_like(local_state))
    carried = carried_in((device_decay, local_state), "ctx", combine_pairs, identity_pair)[1]
    block_index = jnp.arange(block_count, dtype=jnp.float32)
    block_starts = jnp.exp(-decay_rate[None, :, :] * (block_index[:, None, None] * block_rows))
    coefficient = block_starts * (residues * carried)[None, :, :]
    correction = jnp.einsum("rcm,bcm->brc", entry_powers, coefficient).reshape(row_count, channels)
    untouched = (ages > local_index).astype(jnp.float32)[:, None]
    filtered = within + between.reshape(row_count, channels) + correction * untouched
    gated = (query_conv * filtered).astype(jnp.bfloat16)
    all_channels = lax.all_gather(gated, "ch", axis=1, tiled=True)
    result = jnp.dot(
        all_channels,
        lax.all_gather(out_weight, "ctx", axis=0, tiled=True),
        preferred_element_type=jnp.float32,
    )
    return result.astype(jnp.bfloat16)


def solution(mesh):
    return jax.shard_map(
        local,
        mesh=mesh,
        in_specs=(
            P("ctx", "ch"),
            P("ctx", "ch"),
            P("ctx", "ch"),
            P(None, None, "ch"),
            P("ch", None),
            P("ch", None),
            P("ctx", "ch"),
            P(),
        ),
        out_specs=P("ctx", "ch"),
        check_vma=False,
    )
```

profile of v0, /device:TPU:32, one launch (start us, length us, event | category | flops | bytes accessed | tf_op | source)
XLA Modules:
  0.0 616.6 jit_solution(5873278730106274515)
XLA Ops:
  7.3 3.8 collective-permute-start.1
  11.8 3.8 collective-permute-start.2
  17.6 1.6 fusion.59
  23.6 2.8 copy.59
  26.3 5.7 fusion.16
  32.1 5.2 copy.61
  37.3 32.3 %while.27 = (s32[]{:T(128)}, f32[1024,16]{0,1:T(8,128)S(1)}, f32[16,1024,16]{1,2,0:T(8,128)}, f32[16]{0:T(128)S(1)}, f32[1024,16]{0,1:T(8,128)S(1)}, /*index=5*/f32[16,1024,16]{1,2,0:T(8,128)S(1)}, s32[]{:T(128)}, s32[]{:T(128)}) while((s32[]{:T(128)}, f32[1024,16]{0,1:T(8,128)S(1)}, f32[16,1024,16]{1,2,0:T(8,128)}, ...), condition=%wide.region_3.4_spmd.clone, body=%wide.region_2.3_spmd.clone.sunk | while | flops 81923 | bytes 393844 | solution.py:117
  70.3 5.0 collective-permute-start
  76.8 2.1 slice_reduce_fusion.7
  79.1 4.9 copy.62
  84.0 6.5 %multiply_bitcast_fusion = f32[16,8,1024]{0,1,2:T(8,128)} fusion(bf16[16,1024,16]{2,0,1:T(8,128)(2,1)} %copy.62, f32[16,8]{0,1:T(8,128)S(1)} %copy.63, f32[8]{0:T(128)S(1)} %iota_add_fusion, f32[1024,16]{1,0:T(8,128)S(1)} %copy.57), kind=kOutput, calls=%fused_computation.16 | convolution fusion | flops 4456448 | bytes 1114656 | tf_op jit(solution)/shard_map/rcm,bcm->brc/dot_general | solution.py:122
  90.5 3.0 copy.64
  93.6 74.4 %all-gather.11.cloned.1.call-done = f32[65536,16]{0,1:T(8,128)} async-done(((f32[1024,16]{0,1:T(8,128)}), f32[65536,16]{0,1:T(8,128)}) %all-gather.11.cloned.1.call-update) | async-done | bytes 4194320 | tf_op jit(solution)/shard_map/all_gather | solution.py:18
  168.0 6.5 %copy.72 = f32[2,8,64,1024]{3,2,1,0:T(8,128)} copy(f32[2,8,64,1024]{3,1,2,0:T(8,128)} %bitcast.68) | data formatting | bytes 8388608
  174.5 137.7 %all-gather.13.cloned.1.call-done = f32[65536,16]{0,1:T(8,128)} async-done(((f32[1024,16]{0,1:T(8,128)}), f32[65536,16]{0,1:T(8,128)}) %all-gather.13.cloned.1.call-update) | async-done | bytes 4194320 | tf_op jit(solution)/shard_map/all_gather | solution.py:18
  312.3 6.6 %copy.73 = f32[2,8,64,1024]{3,2,1,0:T(8,128)} copy(f32[2,8,64,1024]{3,1,2,0:T(8,128)} %bitcast.69) | data formatting | bytes 8388608
  318.9 88.1 %while.28 = (s32[]{:T(128)}, f32[1024,16]{0,1:T(8,128)S(1)}, s32[]{:T(128)}, f32[64,1024,16]{1,0,2:T(8,128)}, f32[64,1024,16]{1,0,2:T(8,128)}, /*index=5*/s32[]{:T(128)}, s32[]{:T(128)}) while((s32[]{:T(128)}, f32[1024,16]{0,1:T(8,128)S(1)}, s32[]{:T(128)}, f32[64,1024,16]{1,0,2:T(8,128)}, f32[64,1024,16]{1,0,2:T(8,128)}, ...), condition=%wide.region_5.6_spmd.clone, body=%wide.region_4.5_spmd.clone.sunk | while | flops 65540 | bytes 524389 | solution.py:28
  320.2 1.3 constant_dynamic-slice_fusion.3
  321.6 1.3 constant_dynamic-slice_fusion.3
  323.0 1.3 constant_dynamic-slice_fusion.3
  324.4 1.3 constant_dynamic-slice_fusion.3
  325.7 1.3 constant_dynamic-slice_fusion.3
  327.1 1.3 constant_dynamic-slice_fusion.3
  328.5 1.3 constant_dynamic-slice_fusion.3
  329.9 1.3 constant_dynamic-slice_fusion.3
  331.2 1.3 constant_dynamic-slice_fusion.3
  332.6 1.3 constant_dynamic-slice_fusion.3
  334.0 1.3 constant_dynamic-slice_fusion.3
  335.4 1.3 constant_dynamic-slice_fusion.3
  338.1 1.3 constant_dynamic-slice_fusion.3
  339.5 1.3 constant_dynamic-slice_fusion.3
  340.9 1.3 constant_dynamic-slice_fusion.3
  342.3 1.3 constant_dynamic-slice_fusion.3
  345.0 1.3 constant_dynamic-slice_fusion.3
  346.4 1.3 constant_dynamic-slice_fusion.3
  347.8 1.3 constant_dynamic-slice_fusion.3
  349.1 1.3 constant_dynamic-slice_fusion.3
  350.5 1.3 constant_dynamic-slice_fusion.3
  351.9 1.3 constant_dynamic-slice_fusion.3
  353.3 1.3 constant_dynamic-slice_fusion.3
  354.6 1.3 constant_dynamic-slice_fusion.3
  356.0 1.3 constant_dynamic-slice_fusion.3
  357.4 1.3 constant_dynamic-slice_fusion.3
  358.8 1.3 constant_dynamic-slice_fusion.3
  360.1 1.3 constant_dynamic-slice_fusion.3
  361.5 1.3 constant_dynamic-slice_fusion.3
  364.3 1.3 constant_dynamic-slice_fusion.3
  365.6 1.3 constant_dynamic-slice_fusion.3
  367.0 1.3 constant_dynamic-slice_fusion.3
  368.4 1.3 constant_dynamic-slice_fusion.3
  371.2 1.3 constant_dynamic-slice_fusion.3
  372.5 1.3 constant_dynamic-slice_fusion.3
  373.9 1.3 constant_dynamic-slice_fusion.3
  375.3 1.3 constant_dynamic-slice_fusion.3
  376.7 1.3 constant_dynamic-slice_fusion.3
  378.0 1.3 constant_dynamic-slice_fusion.3
  379.4 1.3 constant_dynamic-slice_fusion.3
  380.8 1.3 constant_dynamic-slice_fusion.3
  407.2 3.9 fusion.21
  411.0 3.0 copy.69
  414.0 1.7 fusion.47
  416.3 27.3 %all-gather.7.cloned.1.call-done = bf16[128,8192]{1,0:T(8,128)(2,1)} async-done(((bf16[128,1024]{1,0:T(8,128)(2,1)}), bf16[128,8192]{1,0:T(8,128)(2,1)}) %all-gather.7.cloned.1.call-update) | async-done | bytes 2097168 | tf_op jit(solution)/shard_map/all_gather | solution.py:137
  443.7 160.5 %all-gather.9.cloned.1.call-done = bf16[8192,512]{1,0:T(8,128)(2,1)} async-done(((bf16[128,512]{1,0:T(8,128)(2,1)}), bf16[8192,512]{1,0:T(8,128)(2,1)}) %all-gather.9.cloned.1.call-update) | async-done | bytes 8388624 | tf_op jit(solution)/shard_map/all_gather | solution.py:140
  604.1 5.9 convolution_convert_fusion
  (187 shorter events, 74.9 us)
Async XLA Ops:
  6.5 161.5 %all-gather.11.cloned.1.call-start = ((), (), s32[]{:S(2)}) async-start(), calls=%async_computation.2 | async-start | bytes 4259840 | tf_op jit(solution)/shard_map/all_gather | solution.py:18
  7.3 13.7 %collective-permute-start.1 = (bf16[2,1024]{1,0:T(2,128)(2,1)S(1)}, bf16[2,1024]{1,0:T(2,128)(2,1)S(1)}, u32[]{:S(2)}, u32[]{:S(2)}) collective-permute-start(bf16[2,1024]{1,0:T(2,128)(2,1)S(1)} %slice.146), channel_id=1, source_target_pairs={{0,8},{8,16},{16,24},{24,32},{32,40},{40,48},{48,56},{56,64},{64,7... | collective-permute-start | bytes 12296 | tf_op jit(solution)/shard_map/ppermute | solution.py:13
  11.8 10.2 %collective-permute-start.2 = (bf16[2,1024]{1,0:T(2,128)(2,1)S(1)}, bf16[2,1024]{1,0:T(2,128)(2,1)S(1)}, u32[]{:S(2)}, u32[]{:S(2)}) collective-permute-start(bf16[2,1024]{1,0:T(2,128)(2,1)S(1)} %slice.153), channel_id=1, source_target_pairs={{0,8},{8,16},{16,24},{24,32},{32,40},{40,48},{48,56},{56,64},{64,7... | collective-permute-start | bytes 12296 | tf_op jit(solution)/shard_map/ppermute | solution.py:13
  19.2 293.1 %all-gather.13.cloned.1.call-start = ((), (), s32[]{:S(2)}) async-start(), calls=%async_computation.3 | async-start | bytes 4259840 | tf_op jit(solution)/shard_map/all_gather | solution.py:18
  32.1 38.2 %copy-start.3 = (bf16[128,1024]{1,0:T(8,128)(2,1)S(1)}, bf16[128,1024]{1,0:T(8,128)(2,1)}, u32[]{:S(2)}) copy-start(bf16[128,1024]{1,0:T(8,128)(2,1)} %param.12) | copy-start | bytes 786436
  37.3 41.7 %copy-start.2 = (f32[1024,16]{0,1:T(8,128)S(1)}, f32[1024,16]{0,1:T(8,128)}, u32[]{:S(2)}) copy-start(f32[1024,16]{0,1:T(8,128)} %param.17) | copy-start | bytes 196612
  69.6 0.6 copy-start
  69.6 9.4 %copy-start.1 = (f32[16,1024,16]{1,2,0:T(8,128)S(1)}, f32[16,1024,16]{1,2,0:T(8,128)}, u32[]{:S(2)}) copy-start(f32[16,1024,16]{1,2,0:T(8,128)} %get-tuple-element.132) | copy-start | bytes 3145732
  70.2 373.5 %all-gather.7.cloned.1.call-start = ((), (), s32[]{:S(2)}) async-start(), calls=%async_computation | async-start | bytes 2359296 | tf_op jit(solution)/shard_map/all_gather | solution.py:137
  70.3 23.2 %collective-permute-start = (bf16[2,1024]{1,0:T(2,128)(2,1)S(1)}, bf16[2,1024]{1,0:T(2,128)(2,1)S(1)}, u32[]{:S(2)}, u32[]{:S(2)}) collective-permute-start(bf16[2,1024]{1,0:T(2,128)(2,1)S(1)} %slice.138), channel_id=1, source_target_pairs={{0,8},{8,16},{16,24},{24,32},{32,40},{40,48},{48,56},{56,64},{64,7... | collective-permute-start | bytes 12296 | tf_op jit(solution)/shard_map/ppermute | solution.py:13
  415.8 188.4 %all-gather.9.cloned.1.call-start = ((), (), s32[]{:S(2)}) async-start(), calls=%async_computation.1 | async-start | bytes 8519680 | tf_op jit(solution)/shard_map/all_gather | solution.py:140
Sparse Core Ops, SparseCore 0:
  19.3 148.6 all-gather.10
  171.0 141.2 all-gather.12
  415.9 27.7 all-gather.6
  446.5 157.6 all-gather.8
where the time goes:
time: 619 us; the launch traced here: 617 us
  waiting for transfers between devices  401 us (65%)
  local copies, waits for them, and re-layouts  133 us (21%)
  other arithmetic  32.3 us (5%)
  matrix products  22.1 us (4%)
  between operations  14.1 us (2%)
  starting transfers between devices  12.8 us (2%)
    all_gather x2, waiting for transfers between devices, carried_in(): everything = jax.tree.map(lambda part: lax.all_gather(part, axis), x)  212 us
    all_gather x1, waiting for transfers between devices, local(): lax.all_gather(out_weight, 'ctx', axis=0, tiled=True)  160 us
    dynamic_slice x64, local copies, waits for them, and re-layouts, hop(): new = combine(before, jax.tree.map(lambda part: part[k], everything))  83.4 us
    all_gather x1, waiting for transfers between devices, local(): all_channels = lax.all_gather(gated, 'ch', axis=1, tiled=True)  27.3 us
    unnamed x11, local copies, waits for them, and re-layouts  18.9 us
    ppermute x3, starting transfers between devices, shifted(): return lax.ppermute(block, axis, route)  12.7 us
  transfers between devices with their start and end apart: 7, of which 4 were waited for; matrix products, arithmetic and copies ran while one was open for 13% of the time, Pallas kernels for 0%

commit v1 on v0

--- a/solution.py
+++ b/solution.py
@@ -134,7 +134,9 @@
     untouched = (ages > local_index).astype(jnp.float32)[:, None]
     filtered = within + between.reshape(row_count, channels) + correction * untouched
     gated = (query_conv * filtered).astype(jnp.bfloat16)
-    all_channels = lax.all_gather(gated, "ch", axis=1, tiled=True)
+    all_channels = jnp.concatenate(
+        lax.all_to_all(jnp.stack([gated] * lax.axis_size("ch")), "ch", 0, 0), axis=1
+    )
     result = jnp.dot(
         all_channels,
         lax.all_gather(out_weight, "ctx", axis=0, tiled=True),

time: 619 us -> 482 us (0.78)
  the two profiles are of different devices: /device:TPU:32 before, /device:TPU:2 now
where the time goes in v1:
time: 482 us; the launch traced here: 479 us
  waiting for transfers between devices  236 us (49%)
  local copies, waits for them, and re-layouts  133 us (28%)
  other arithmetic  30.7 us (6%)
  blocking collectives  30.7 us (6%)
  matrix products  21.5 us (4%)
  between operations  14.1 us (3%)
  starting transfers between devices  11.5 us (2%)
    all_gather x2, waiting for transfers between devices, carried_in(): everything = jax.tree.map(lambda part: lax.all_gather(part, axis), x)  216 us
    dynamic_slice x64, local copies, waits for them, and re-layouts, hop(): new = combine(before, jax.tree.map(lambda part: part[k], everything))  83.6 us
    all_to_all x1, blocking collectives, local(): lax.all_to_all(jnp.stack([gated] * lax.axis_size('ch')), 'ch', 0, 0)  30.7 us
    all_gather x1, waiting for transfers between devices, local(): lax.all_gather(out_weight, 'ctx', axis=0, tiled=True)  20 us
    unnamed x11, local copies, waits for them, and re-layouts  19 us
    ppermute x3, starting transfers between devices, shifted(): return lax.ppermute(block, axis, route)  11.4 us
    add x16, other arithmetic, advance(): return (block_decay * kept * state + ending, state)  10.4 us
    dynamic_update_slice x16, other arithmetic, local(): lax.scan(advance, jnp.zeros((channels, MODES), jnp.float32), (endings, un...  10 us
  transfers between devices with their start and end apart: 6, of which 3 were waited for; matrix products, arithmetic and copies ran while one was open for 37% of the time, Pallas kernels for 0%

profile of v1, /device:TPU:2, one launch (start us, length us, event | category | flops | bytes accessed | tf_op | source)
XLA Modules:
  0.0 479.3 jit_solution(13294364404282448633)
XLA Ops:
  7.3 3.8 collective-permute-start.1
  11.8 3.8 collective-permute-start.2
  17.6 1.6 fusion.59
  23.6 2.8 copy.62
  26.3 5.7 %fusion.16 = f32[16,1024,16]{2,0,1:T(8,128)} fusion(f32[16,8,1024]{0,1,2:T(8,128)} %copy.62, f32[1024,16]{1,0:T(8,128)S(1)} %copy.63, f32[8]{0:T(128)S(1)} %iota_subtract_fusion, f32[16,8]{0,1:T(8,128)S(1)} %compare_convert_fusion, f32[1024,16]{1,0:T(8,128)S(1)} %copy.60), kind=kOutput, calls=%fused_computation.25 | convolution fusion | flops 4587520 | bytes 1704480 | tf_op jit(solution)/shard_map/rcm,brc->bcm/dot_general | solution.py:110
  32.1 5.2 %copy.64 = f32[16,1024,16]{1,2,0:T(8,128)S(1)} copy(f32[16,1024,16]{2,0,1:T(8,128)} %fusion.16) | data formatting | bytes 2097152
  37.3 30.5 %while.27 = (s32[]{:T(128)}, f32[1024,16]{0,1:T(8,128)S(1)}, f32[16,1024,16]{1,2,0:T(8,128)}, f32[16]{0:T(128)S(1)}, f32[1024,16]{0,1:T(8,128)S(1)}, /*index=5*/f32[16,1024,16]{1,2,0:T(8,128)S(1)}, s32[]{:T(128)}, s32[]{:T(128)}) while((s32[]{:T(128)}, f32[1024,16]{0,1:T(8,128)S(1)}, f32[16,1024,16]{1,2,0:T(8,128)}, ...), condition=%wide.region_3.4_spmd.clone, body=%wide.region_2.3_spmd.clone.sunk | while | flops 81923 | bytes 393844 | solution.py:117
  68.5 3.8 collective-permute-start
  73.9 2.1 slice_reduce_fusion.7
  76.2 4.9 %copy.65 = bf16[16,1024,16]{2,0,1:T(8,128)(2,1)} copy(bf16[16,1024,16]{1,2,0:T(8,128)(2,1)S(1)} %broadcast_multiply_fusion) | data formatting | bytes 1048576 | tf_op jit(solution)/shard_map/mul | solution.py:122
  81.1 6.5 %multiply_bitcast_fusion = f32[16,8,1024]{0,1,2:T(8,128)} fusion(bf16[16,1024,16]{2,0,1:T(8,128)(2,1)} %copy.65, f32[16,8]{0,1:T(8,128)S(1)} %copy.66, f32[8]{0:T(128)S(1)} %iota_add_fusion, f32[1024,16]{1,0:T(8,128)S(1)} %copy.60), kind=kOutput, calls=%fused_computation.16 | convolution fusion | flops 4456448 | bytes 1114656 | tf_op jit(solution)/shard_map/rcm,bcm->brc/dot_general | solution.py:122
  87.6 3.0 copy.67
  90.7 78.0 %all-gather.8.cloned.1.call-done = f32[65536,16]{0,1:T(8,128)} async-done(((f32[1024,16]{0,1:T(8,128)}), f32[65536,16]{0,1:T(8,128)}) %all-gather.8.cloned.1.call-update) | async-done | bytes 4194320 | tf_op jit(solution)/shard_map/all_gather | solution.py:18
  168.6 6.6 %copy.76 = f32[2,8,64,1024]{3,2,1,0:T(8,128)} copy(f32[2,8,64,1024]{3,1,2,0:T(8,128)} %bitcast.72) | data formatting | bytes 8388608
  175.2 137.7 %all-gather.10.cloned.1.call-done = f32[65536,16]{0,1:T(8,128)} async-done(((f32[1024,16]{0,1:T(8,128)}), f32[65536,16]{0,1:T(8,128)}) %all-gather.10.cloned.1.call-update) | async-done | bytes 4194320 | tf_op jit(solution)/shard_map/all_gather | solution.py:18
  312.9 6.6 %copy.77 = f32[2,8,64,1024]{3,2,1,0:T(8,128)} copy(f32[2,8,64,1024]{3,1,2,0:T(8,128)} %bitcast.73) | data formatting | bytes 8388608
  319.5 88.3 %while.28 = (s32[]{:T(128)}, f32[1024,16]{0,1:T(8,128)S(1)}, s32[]{:T(128)}, f32[64,1024,16]{1,0,2:T(8,128)}, f32[64,1024,16]{1,0,2:T(8,128)}, /*index=5*/s32[]{:T(128)}, s32[]{:T(128)}) while((s32[]{:T(128)}, f32[1024,16]{0,1:T(8,128)S(1)}, s32[]{:T(128)}, f32[64,1024,16]{1,0,2:T(8,128)}, f32[64,1024,16]{1,0,2:T(8,128)}, ...), condition=%wide.region_5.6_spmd.clone, body=%wide.region_4.5_spmd.clone.sunk | while | flops 65540 | bytes 524389 | solution.py:28
  320.9 1.3 constant_dynamic-slice_fusion.3
  322.3 1.3 constant_dynamic-slice_fusion.3
  323.6 1.3 constant_dynamic-slice_fusion.3
  325.0 1.3 constant_dynamic-slice_fusion.3
  326.4 1.3 constant_dynamic-slice_fusion.3
  329.1 1.3 constant_dynamic-slice_fusion.3
  330.5 1.3 constant_dynamic-slice_fusion.3
  331.9 1.3 constant_dynamic-slice_fusion.3
  333.3 1.3 constant_dynamic-slice_fusion.3
  334.6 1.3 constant_dynamic-slice_fusion.3
  336.0 1.3 constant_dynamic-slice_fusion.3
  337.4 1.3 constant_dynamic-slice_fusion.3
  338.8 1.3 constant_dynamic-slice_fusion.3
  340.2 1.3 constant_dynamic-slice_fusion.3
  341.5 1.3 constant_dynamic-slice_fusion.3
  342.9 1.3 constant_dynamic-slice_fusion.3
  344.3 1.3 constant_dynamic-slice_fusion.3
  345.7 1.3 constant_dynamic-slice_fusion.3
  347.0 1.3 constant_dynamic-slice_fusion.3
  348.4 1.3 constant_dynamic-slice_fusion.3
  349.8 1.3 constant_dynamic-slice_fusion.3
  351.2 1.3 constant_dynamic-slice_fusion.3
  352.6 1.3 constant_dynamic-slice_fusion.3
  354.0 1.3 constant_dynamic-slice_fusion.3
  355.3 1.3 constant_dynamic-slice_fusion.3
  356.7 1.3 constant_dynamic-slice_fusion.3
  358.1 1.3 constant_dynamic-slice_fusion.3
  359.5 1.3 constant_dynamic-slice_fusion.3
  360.8 1.3 constant_dynamic-slice_fusion.3
  362.2 1.3 constant_dynamic-slice_fusion.3
  363.6 1.3 constant_dynamic-slice_fusion.3
  365.0 1.3 constant_dynamic-slice_fusion.3
  367.7 1.3 constant_dynamic-slice_fusion.3
  369.1 1.3 constant_dynamic-slice_fusion.3
  370.5 1.3 constant_dynamic-slice_fusion.3
  371.9 1.3 constant_dynamic-slice_fusion.3
  373.3 1.3 constant_dynamic-slice_fusion.3
  377.4 1.3 constant_dynamic-slice_fusion.3
  396.7 1.4 constant_dynamic-slice_fusion.3
  402.3 1.3 constant_dynamic-slice_fusion.3
  403.6 1.3 constant_dynamic-slice_fusion.3
  406.4 1.3 constant_dynamic-slice_fusion.3
  408.1 3.9 fusion.21
  411.9 3.3 copy.72
  416.7 30.7 %all_to_all.5 = bf16[8,128,1024]{1,2,0:T(8,128)(2,1)S(1)} all-to-all(bf16[8,128,1024]{1,2,0:T(8,128)(2,1)S(1)} %stack.2), channel_id=1, replica_groups=mesh['ctx'=64,'ch'=8] {'ch'}, dimensions={0} | all-to-all | bytes 4194304 | tf_op jit(solution)/shard_map/all_to_all | solution.py:138
  447.4 20.0 %all-gather.6.cloned.1.call-done = bf16[8192,512]{1,0:T(8,128)(2,1)} async-done(((bf16[128,512]{1,0:T(8,128)(2,1)}), bf16[8192,512]{1,0:T(8,128)(2,1)}) %all-gather.6.cloned.1.call-update) | async-done | bytes 8388624 | tf_op jit(solution)/shard_map/all_gather | solution.py:142
  467.4 5.3 %convolution_convert_fusion = bf16[128,512]{1,0:T(8,128)(2,1)} fusion(bf16[128,8192]{0,1:T(8,128)(2,1)S(1)} %bitcast.68, bf16[8192,512]{1,0:T(8,128)(2,1)} %all-gather.6.cloned.1.call-done), kind=kOutput, calls=%fused_computation.35 | convolution fusion | flops 1073807360 | bytes 10616832 | tf_op jit(solution)/shard_map/dot_general | solution.py:140
  (187 shorter events, 72.8 us)
Async XLA Ops:
  6.5 162.1 %all-gather.8.cloned.1.call-start = ((), (), s32[]{:S(2)}) async-start(), calls=%async_computation.2 | async-start | bytes 4259840 | tf_op jit(solution)/shard_map/all_gather | solution.py:18
  7.3 13.7 %collective-permute-start.1 = (bf16[2,1024]{1,0:T(2,128)(2,1)S(1)}, bf16[2,1024]{1,0:T(2,128)(2,1)S(1)}, u32[]{:S(2)}, u32[]{:S(2)}) collective-permute-start(bf16[2,1024]{1,0:T(2,128)(2,1)S(1)} %slice.146), channel_id=1, source_target_pairs={{0,8},{8,16},{16,24},{24,32},{32,40},{40,48},{48,56},{56,64},{64,7... | collective-permute-start | bytes 12296 | tf_op jit(solution)/shard_map/ppermute | solution.py:13
  11.8 10.2 %collective-permute-start.2 = (bf16[2,1024]{1,0:T(2,128)(2,1)S(1)}, bf16[2,1024]{1,0:T(2,128)(2,1)S(1)}, u32[]{:S(2)}, u32[]{:S(2)}) collective-permute-start(bf16[2,1024]{1,0:T(2,128)(2,1)S(1)} %slice.153), channel_id=1, source_target_pairs={{0,8},{8,16},{16,24},{24,32},{32,40},{40,48},{48,56},{56,64},{64,7... | collective-permute-start | bytes 12296 | tf_op jit(solution)/shard_map/ppermute | solution.py:13
  19.2 293.7 %all-gather.10.cloned.1.call-start = ((), (), s32[]{:S(2)}) async-start(), calls=%async_computation.3 | async-start | bytes 4259840 | tf_op jit(solution)/shard_map/all_gather | solution.py:18
  32.1 36.4 %copy-start.3 = (bf16[128,1024]{1,0:T(8,128)(2,1)S(1)}, bf16[128,1024]{1,0:T(8,128)(2,1)}, u32[]{:S(2)}) copy-start(bf16[128,1024]{1,0:T(8,128)(2,1)} %param.12) | copy-start | bytes 786436
  37.3 38.8 %copy-start.2 = (f32[1024,16]{0,1:T(8,128)S(1)}, f32[1024,16]{0,1:T(8,128)}, u32[]{:S(2)}) copy-start(f32[1024,16]{0,1:T(8,128)} %param.17) | copy-start | bytes 196612
  67.8 0.6 copy-start
  67.8 8.2 %copy-start.1 = (f32[16,1024,16]{1,2,0:T(8,128)S(1)}, f32[16,1024,16]{1,2,0:T(8,128)}, u32[]{:S(2)}) copy-start(f32[16,1024,16]{1,2,0:T(8,128)} %get-tuple-element.132) | copy-start | bytes 3145732
  68.5 398.9 %all-gather.6.cloned.1.call-start = ((), (), s32[]{:S(2)}) async-start(), calls=%async_computation.1 | async-start | bytes 8519680 | tf_op jit(solution)/shard_map/all_gather | solution.py:142
  68.5 22.1 %collective-permute-start = (bf16[2,1024]{1,0:T(2,128)(2,1)S(1)}, bf16[2,1024]{1,0:T(2,128)(2,1)S(1)}, u32[]{:S(2)}, u32[]{:S(2)}) collective-permute-start(bf16[2,1024]{1,0:T(2,128)(2,1)S(1)} %slice.138), channel_id=1, source_target_pairs={{0,8},{8,16},{16,24},{24,32},{32,40},{40,48},{48,56},{56,64},{64,7... | collective-permute-start | bytes 12296 | tf_op jit(solution)/shard_map/ppermute | solution.py:13
Sparse Core Ops, SparseCore 0:
  19.3 149.2 all-gather.7
  171.6 141.2 all-gather.9
  315.9 151.4 all-gather.5
